TPU v7x, 32 devices: a whole 2x2x4 slice. The times are simulated.
32 devices in a mesh: outer: 4 (over y, x), inner: 8 (over z, core).
Axes of the slice: x: 2, y: 2, z: 4, core: 2. Of those that a mesh axis runs over, the one named last changes fastest.
Arguments:
- queries: bfloat16 [49152, 2048], P(('outer', 'inner')), may hold values from -6 to 6
- keys: bfloat16 [49152, 2048], P(('outer', 'inner')), may hold values from -6 to 6
- values: bfloat16 [49152, 2048], P(('outer', 'inner')), may hold values from -6 to 6
- gain: float32 [2048], replicated, may hold values from 0.5 to 1.5
- tile_doc: int32 [384], P(('outer', 'inner')), may hold values from 0 to 7, as said below
- tile_fill: int32 [384], P(('outer', 'inner')), may hold values from 1 to 128, as said below
Outputs:
- attended: bfloat16 [49152, 2048], P(('outer', 'inner'))
Inputs may be any that keep to these rules, and one draw needn't show every extreme that they name: tile_doc is 0 at the first tile and rises by 0 or 1 from each tile to the next, so each document holds whole consecutive tiles; the window holds exactly 8 documents. tile_fill is 128 on every tile except the last tile of each document.
All inputs are finite; a program needn't handle non-finite values.
Results may differ from a plain program's by a relative error of at most 0.0027.
Values sent between devices are 32-bit elements; how exact they have to be, the bound alone decides.
A program may use at most 192 MiB of HBM per device.

v0:
```python
from functools import reduce
import jax
import jax.numpy as jnp
from jax import lax
from jax.sharding import PartitionSpec as P

HEADS = 16
HEAD = 128
TILE = 128
BLOCK = 512


def shifted(value, axis, by):
    length = lax.axis_size(axis)
    pairs = [(i, i + by) for i in range(length) if 0 <= i + by < length]
    return lax.ppermute(value, axis, pairs)


def entering(value, axis, join, neutral):
    count, mine = (lax.axis_size(axis), lax.axis_index(axis))
    pieces = jax.tree.map(lambda part: lax.all_gather(part, axis), value)
    so_far = jax.tree.map(
        lambda part, zero: jnp.full_like(part, 0) + jnp.asarray(zero, part.dtype), value, neutral
    )

    def lap(position, so_far):
        longer = join(so_far, jax.tree.map(lambda part: part[position], pieces))
        return jax.tree.map(lambda new, old: jnp.where(position < mine, new, old), longer, so_far)

    return lax.fori_loop(0, count - 1, lap, so_far)


def spread(value, axis, source):
    kept = jnp.where(lax.axis_index(axis) == source, value, 0).astype(value.dtype)
    return lax.psum(kept, axis)


def combine(first, second):
    first_state, first_last, first_single = first
    second_state, second_last, second_single = second
    second_none = second_last[0] == 0
    first_none = first_last[0] == 0
    keep = jnp.logical_or(
        second_none, jnp.logical_and(second_single[0] == 1, second_last[0] == first_last[0])
    )
    state = jnp.where(keep, second_state + first_state, second_state)
    last = jnp.where(second_none, first_last, second_last)
    same = (first_last == second_last).astype(jnp.int32)
    single = jnp.where(
        second_none,
        first_single,
        jnp.where(first_none, second_single, first_single * second_single * same),
    )
    return (state, last, single)


def summarize(key_rows, value_rows, docs, real):
    last_doc = docs[-1]
    chosen = jnp.logical_and(docs == last_doc, real)
    masked = jnp.where(chosen[:, None, None], key_rows, jnp.zeros_like(key_rows))
    state = jnp.einsum("thd,the->hde", masked, value_rows, preferred_element_type=jnp.float32)
    last = (last_doc + 1).reshape(1)
    single = (docs[0] == last_doc).astype(jnp.int32).reshape(1)
    return (state, last, single)


def direct_part(query_rows, key_rows, value_rows, docs, real):
    length = query_rows.shape[0]
    scores = jnp.einsum("qhd,khd->hqk", query_rows, key_rows, preferred_element_type=jnp.float32)
    places = jnp.arange(length)
    allowed = (
        (places[:, None] >= places[None, :]) & (docs[:, None] == docs[None, :]) & real[None, :]
    )
    weights = jnp.where(allowed[None], scores, 0.0).astype(jnp.bfloat16)
    return jnp.einsum("hqk,khd->qhd", weights, value_rows, preferred_element_type=jnp.float32)


def finish(direct, query_rows, docs, real, carry, gain):
    state, last, single = carry
    carried = jnp.einsum(
        "qhd,hde->qhe", query_rows.astype(jnp.float32), state, precision=lax.Precision.HIGHEST
    )
    uses = docs + 1 == last[0]
    raw = direct + jnp.where(uses[:, None, None], carried, 0.0)
    raw = jnp.where(real[:, None, None], raw, 0.0)
    meansq = jnp.mean(raw * raw, axis=-1, keepdims=True)
    normed = raw * lax.rsqrt(meansq + 1e-06) * gain.reshape(HEADS, HEAD)
    return normed.astype(jnp.bfloat16).reshape(query_rows.shape[0], HEADS * HEAD)


def empty_state():
    return (
        jnp.zeros((HEADS, HEAD, HEAD), jnp.float32),
        jnp.zeros((1,), jnp.int32),
        jnp.zeros((1,), jnp.int32),
    )


def across_groups(total):
    earlier = empty_state()
    for step in range(lax.axis_size("outer") - 1):
        running = combine(earlier, total)
        earlier = shifted((running[0], running[1], running[2]), "outer", 1)
    return earlier


def body(queries, keys, values, gain, tile_doc, tile_fill):
    length = queries.shape[0]
    count = length // BLOCK
    docs = jnp.repeat(tile_doc, TILE)
    real = jnp.arange(length, dtype=jnp.int32) % TILE < jnp.repeat(tile_fill, TILE)
    query_all = queries.reshape(length, HEADS, HEAD)
    key_all = keys.reshape(length, HEADS, HEAD)
    value_all = values.reshape(length, HEADS, HEAD)
    directs = []
    summaries = []
    for block in range(count):
        lower = block * BLOCK
        upper = lower + BLOCK
        directs.append(
            direct_part(
                query_all[lower:upper],
                key_all[lower:upper],
                value_all[lower:upper],
                docs[lower:upper],
                real[lower:upper],
            )
        )
        summaries.append(
            summarize(
                key_all[lower:upper], value_all[lower:upper], docs[lower:upper], real[lower:upper]
            )
        )
    own = reduce(combine, summaries)
    before_inner = entering(own, "inner", combine, empty_state())
    through = combine(before_inner, own)
    total = (
        spread(through[0], "inner", lax.axis_size("inner") - 1),
        spread(through[1], "inner", lax.axis_size("inner") - 1),
        spread(through[2], "inner", lax.axis_size("inner") - 1),
    )
    prefix = combine(across_groups(total), before_inner)
    carry = prefix
    results = []
    for block in range(count):
        lower = block * BLOCK
        upper = lower + BLOCK
        results.append(
            finish(
                directs[block],
                query_all[lower:upper],
                docs[lower:upper],
                real[lower:upper],
                carry,
                gain,
            )
        )
        carry = combine(carry, summaries[block])
    return jnp.concatenate(results, axis=0)


def solution(mesh):
    placed = (
        P(("outer", "inner"), None),
        P(("outer", "inner"), None),
        P(("outer", "inner"), None),
        P(),
        P(("outer", "inner")),
        P(("outer", "inner")),
    )
    return jax.shard_map(
        body, mesh=mesh, in_specs=placed, out_specs=P(("outer", "inner"), None), check_vma=False
    )
```

profile of v0, /device:TPU:4, one launch (start us, length us, event | category | flops | bytes accessed | tf_op | source)
XLA Modules:
  0.0 397.3 jit_solution(3273020750897445659)
XLA Ops:
  16.3 5.9 %fusion.52 = (bf16[512,2048]{1,0:T(8,128)(2,1)}, bf16[512,2048]{1,0:T(8,128)(2,1)S(1)}, bf16[512,2048]{1,0:T(8,128)(2,1)}) fusion(bf16[1536,2048]{1,0:T(8,128)(2,1)} %param.9), kind=kLoop, calls=%fused_computation.91 | loop fusion | bytes 12582912 | tf_op jit(solution)/shard_map/slice | solution.py:123
  22.1 3.9 copy.108
  26.1 5.8 %fusion.53 = (bf16[512,2048]{1,0:T(8,128)(2,1)}, bf16[512,2048]{1,0:T(8,128)(2,1)}, bf16[512,2048]{1,0:T(8,128)(2,1)}) fusion(bf16[1536,2048]{1,0:T(8,128)(2,1)} %param.10), kind=kLoop, calls=%fused_computation.92 | loop fusion | bytes 12582912 | tf_op jit(solution)/shard_map/slice | solution.py:124
  31.9 4.0 copy.69
  35.8 3.9 copy.111
  39.8 3.9 copy.112
  46.2 4.1 %copy.110 = bf16[512,2048]{0,1:T(8,128)(2,1)} copy(bf16[512,2048]{1,0:T(8,128)(2,1)} %get-tuple-element.205) | data formatting | bytes 4194304
  62.0 9.3 %all-reduce.3 = (s32[8]{0:T(128)S(1)}, s32[8]{0:T(128)S(1)}) all-reduce(s32[8]{0:T(128)S(1)} %dynamic-update-slice, s32[8]{0:T(128)S(1)} %dynamic-update-slice.1), channel_id=2, replica_groups=mesh['outer'=4,'inner'=8] {'inner'}, use_global_device_ids=true, to_apply=%add | all-reduce | flops 16 | bytes 128
  71.3 69.7 %all-gather.5.cloned.1.call-done = f32[128,128,128]{2,1,0:T(8,128)} async-done(((f32[16,128,128]{2,1,0:T(8,128)}), f32[128,128,128]{2,1,0:T(8,128)}) %all-gather.5.cloned.1.call-update) | async-done | bytes 8388624 | tf_op jit(solution)/shard_map/all_gather | solution.py:21
  141.0 54.9 %while.18 = (s32[]{:T(128)}, f32[16,128,128]{2,1,0:T(8,128)S(1)}, s32[1]{0:T(128)}, s32[1]{0:T(128)}, s32[]{:T(128)}, /*index=5*/s32[8,1]{0,1:T(1,128)S(1)}, s32...) while((s32[]{:T(128)}, f32[16,128,128]{2,1,0:T(8,128)S(1)}, ...), condition=%wide.region_1.2_spmd.clone, body=%wide.region_0.1_spmd.clone.sunk | while | flops 1048594 | bytes 3146019 | solution.py:30
  197.7 57.4 %all-reduce.6.cloned.1.call-done = f32[16,128,128]{2,1,0:T(8,128)} async-done(((f32[16,128,128]{2,1,0:T(8,128)}), f32[16,128,128]{2,1,0:T(8,128)}) %all-reduce.6.cloned.1.call-update) | async-done | bytes 1048592 | tf_op jit(solution)/shard_map/psum | solution.py:35
  259.5 5.7 %fusion.51 = (bf16[512,2048]{1,0:T(8,128)(2,1)}, bf16[512,2048]{1,0:T(8,128)(2,1)}, bf16[512,2048]{1,0:T(8,128)(2,1)}) fusion(bf16[1536,2048]{1,0:T(8,128)(2,1)} %param.8), kind=kLoop, calls=%fused_computation.90 | loop fusion | bytes 12582912 | tf_op jit(solution)/shard_map/slice | solution.py:122
  269.4 7.8 %all-reduce.2 = (s32[1]{0:T(128)}, s32[1]{0:T(128)}) all-reduce(s32[1]{0:T(128)S(6)} %select_n.305, s32[1]{0:T(128)S(6)} %select_n.313), channel_id=1, replica_groups=mesh['outer'=4,'inner'=8] {'inner'}, use_global_device_ids=true, to_apply=%region_2.3 | all-reduce | flops 2 | bytes 16 | tf_op jit(solution)/shard_map/psum | solution.py:35
  290.7 9.4 %fusion.6 = f32[16,512,128]{1,2,0:T(8,128)} fusion(bf16[512,16,128]{0,2,1:T(8,128)(2,1)} %bitcast.158, bf16[512,16,128]{0,2,1:T(8,128)(2,1)S(1)} %bitcast.138, bf16[512,16,128]{0,2,1:T(8,128)(2,1)} %bitcast.156, pred[512,512]{1,0:T(8,128)(4,1)} %get-tuple-element.236), kind=kOutput, calls=%fused_computation.22 | convolution fusion | flops 2155872256 | bytes 10747904 | tf_op jit(solution)/shard_map/hqk,khd->qhd/dot_general | solution.py:75
  300.1 3.9 copy.113
  304.0 3.9 copy.107
  308.8 10.0 %fusion.5 = f32[16,512,128]{1,2,0:T(8,128)} fusion(bf16[512,16,128]{0,2,1:T(8,128)(2,1)} %bitcast.154, bf16[512,16,128]{0,2,1:T(8,128)(2,1)} %bitcast.142, bf16[512,16,128]{0,2,1:T(8,128)(2,1)} %bitcast.152, pred[512,512]{1,0:T(8,128)(4,1)S(1)} %get-tuple-element.235), kind=kOutput, calls=%fused_computation.21 | convolution fusion | flops 2155872256 | bytes 10747904 | tf_op jit(solution)/shard_map/hqk,khd->qhd/dot_general | solution.py:75
  332.3 10.0 %fusion.4 = f32[16,512,128]{1,2,0:T(8,128)} fusion(bf16[512,16,128]{0,2,1:T(8,128)(2,1)} %bitcast.151, bf16[512,16,128]{0,2,1:T(8,128)(2,1)} %bitcast.140, bf16[512,16,128]{0,2,1:T(8,128)(2,1)} %bitcast.148, pred[512,512]{1,0:T(8,128)(4,1)S(1)} %copy-done.13), kind=kOutput, calls=%fused_computation.20 | convolution fusion | flops 2155872256 | bytes 10747904 | tf_op jit(solution)/shard_map/hqk,khd->qhd/dot_general | solution.py:75
  343.5 8.7 %collective-permute-start.2 = (s32[1]{0:T(128)}, s32[1]{0:T(128)}, u32[]{:S(2)}, u32[]{:S(2)}) collective-permute-start(s32[1]{0:T(128)} %select_n.308), channel_id=1, source_target_pairs={{0,8},{8,16},{16,24},{1,9},{9,17},{17,25},{2,10},{10,18},{18,26},{... | collective-permute-start | bytes 20 | tf_op jit(solution)/shard_map/ppermute | solution.py:16
  359.7 4.1 %multiply_reduce_fusion = (f32[512,16]{0,1:T(8,128)S(1)}, f32[512,16,128]{0,2,1:T(8,128)S(1)}) fusion(bf16[512,16,128]{0,2,1:T(8,128)(2,1)S(1)} %bitcast.139, f32[16,128,128]{2,1,0:T(8,128)} %copy-done.11, f32[16,128,128]{2,1,0:T(8,128)S(1)} %add_select_fusion.2, pred[]{:T(512)S(6)} %or.55, pred[512]{0:T(512)(128)(4,1)S(1)} %get-tuple-element.234, ...), kind=kOutput, calls=%fused_computation.15 | convolution fusion | flops 1616371712 | bytes 12616705 | tf_op jit(solution)/shard_map/qhd,hde->qhe/dot_general | solution.py:80
  366.7 4.0 multiply_reduce_fusion.2
  377.2 4.0 copy.90
  381.1 4.0 copy.91
  385.1 5.4 %pad_maximum_fusion = bf16[1536,2048]{1,0:T(8,128)(2,1)} fusion(bf16[512,2048]{1,0:T(8,128)(2,1)} %copy.91, bf16[512,2048]{1,0:T(8,128)(2,1)} %copy.90, bf16[512,2048]{1,0:T(8,128)(2,1)S(1)} %copy.89), kind=kLoop, calls=%fused_computation.7 | loop fusion | flops 18874368 | bytes 12582912 | tf_op jit(solution)/shard_map/concatenate | solution.py:159
  (103 shorter events, 86.1 us)
Async XLA Ops:
  6.5 134.4 %all-gather.5.cloned.1.call-start = ((), (), s32[]{:S(2)}) async-start(), calls=%async_computation.1 | async-start | bytes 9437184 | tf_op jit(solution)/shard_map/all_gather | solution.py:21
  46.2 4.1 %copy-start.6 = (bf16[512,2048]{0,1:T(8,128)(2,1)S(1)}, bf16[512,2048]{0,1:T(8,128)(2,1)}, u32[]{:S(2)}) copy-start(bf16[512,2048]{0,1:T(8,128)(2,1)} %copy.108) | copy-start | bytes 6291460
  50.2 2.5 copy-start.7
  50.2 2.9 copy-start.8
  52.7 1.1 copy-start.12
  53.1 1.6 copy-start.9
  53.1 2.6 copy-start.10
  53.8 3.6 copy-start.11
  55.7 3.1 copy-start.15
  57.5 197.6 %all-reduce.6.cloned.1.call-start = ((), (), s32[]{:S(2)}) async-start(), calls=%async_computation | async-start | bytes 2097152 | tf_op jit(solution)/shard_map/psum | solution.py:35
  141.0 55.5 %copy-start.5 = (f32[16,128,128]{2,1,0:T(8,128)S(1)}, f32[16,128,128]{2,1,0:T(8,128)}, u32[]{:S(2)}) copy-start(f32[16,128,128]{2,1,0:T(8,128)} %add_select_fusion.7) | copy-start | bytes 3145732
  255.0 30.8 %collective-permute-start.3 = (f32[16,128,128]{2,1,0:T(8,128)}, f32[16,128,128]{2,1,0:T(8,128)}, u32[]{:S(2)}, u32[]{:S(2)}) collective-permute-start(f32[16,128,128]{2,1,0:T(8,128)} %all-reduce.6.cloned.1.call-done), channel_id=1, source_target_pairs={{0,8},{8,16},{16,24},{1,9},{9,17},{17,25},{2,10},{10,18},{18,26},{... | collective-permute-start | bytes 3145736 | tf_op jit(solution)/shard_map/ppermute | solution.py:16
  278.3 6.3 %collective-permute-start = (s32[1]{0:T(128)}, s32[1]{0:T(128)}, u32[]{:S(2)}, u32[]{:S(2)}) collective-permute-start(s32[1]{0:T(128)} %select_n.306), channel_id=1, source_target_pairs={{0,8},{8,16},{16,24},{1,9},{9,17},{17,25},{2,10},{10,18},{18,26},{... | collective-permute-start | bytes 20 | tf_op jit(solution)/shard_map/ppermute | solution.py:16
  288.6 39.1 %collective-permute-start.4 = (f32[16,128,128]{2,1,0:T(8,128)}, f32[16,128,128]{2,1,0:T(8,128)}, u32[]{:S(2)}, u32[]{:S(2)}) collective-permute-start(f32[16,128,128]{2,1,0:T(8,128)} %add_select_fusion.5), channel_id=1, source_target_pairs={{0,8},{8,16},{16,24},{1,9},{9,17},{17,25},{2,10},{10,18},{18,26},{... | collective-permute-start | bytes 3145736 | tf_op jit(solution)/shard_map/ppermute | solution.py:16
  318.8 13.5 %copy-start.13 = (pred[512,512]{1,0:T(8,128)(4,1)S(1)}, pred[512,512]{1,0:T(8,128)(4,1)}, u32[]{:S(2)}) copy-start(pred[512,512]{1,0:T(8,128)(4,1)} %fusion.25) | copy-start | bytes 786436
  320.1 6.3 %collective-permute-start.1 = (s32[1]{0:T(128)}, s32[1]{0:T(128)}, u32[]{:S(2)}, u32[]{:S(2)}) collective-permute-start(s32[1]{0:T(128)} %select_n.307), channel_id=1, source_target_pairs={{0,8},{8,16},{16,24},{1,9},{9,17},{17,25},{2,10},{10,18},{18,26},{... | collective-permute-start | bytes 20 | tf_op jit(solution)/shard_map/ppermute | solution.py:16
  330.4 26.5 %collective-permute-start.5 = (f32[16,128,128]{2,1,0:T(8,128)}, f32[16,128,128]{2,1,0:T(8,128)}, u32[]{:S(2)}, u32[]{:S(2)}) collective-permute-start(f32[16,128,128]{2,1,0:T(8,128)} %add_select_fusion.4), channel_id=1, source_target_pairs={{0,8},{8,16},{16,24},{1,9},{9,17},{17,25},{2,10},{10,18},{18,26},{... | collective-permute-start | bytes 3145736 | tf_op jit(solution)/shard_map/ppermute | solution.py:16
  343.5 11.8 %collective-permute-start.2 = (s32[1]{0:T(128)}, s32[1]{0:T(128)}, u32[]{:S(2)}, u32[]{:S(2)}) collective-permute-start(s32[1]{0:T(128)} %select_n.308), channel_id=1, source_target_pairs={{0,8},{8,16},{16,24},{1,9},{9,17},{17,25},{2,10},{10,18},{18,26},{... | collective-permute-start | bytes 20 | tf_op jit(solution)/shard_map/ppermute | solution.py:16
  356.9 2.8 copy-start.4
  359.7 4.1 %copy-start.2 = (bf16[512,2048]{0,1:T(8,128)(2,1)S(1)}, bf16[512,2048]{0,1:T(8,128)(2,1)}, u32[]{:S(2)}) copy-start(bf16[512,2048]{0,1:T(8,128)(2,1)} %copy.113) | copy-start | bytes 6291460
  359.7 4.1 %copy-start.3 = (f32[16,512,128]{1,2,0:T(8,128)S(1)}, f32[16,512,128]{1,2,0:T(8,128)}, u32[]{:S(2)}) copy-start(f32[16,512,128]{1,2,0:T(8,128)} %fusion.5) | copy-start | bytes 12582916
  363.8 2.6 copy-start
  363.8 2.9 copy-start.1
  366.7 4.0 %copy-start.14 = (f32[2048]{0:T(1024)S(1)}, f32[2048]{0:T(1024)}, u32[]{:S(2)}) copy-start(f32[2048]{0:T(1024)} %param.11) | copy-start | bytes 24580
Sparse Core Ops, SparseCore 0:
  57.6 83.3 all-gather.4
  197.8 57.2 all-reduce.5
where the time goes:
time: 399 us; the launch traced here: 397 us
  waiting for transfers between devices  136 us (34%)
  local copies, waits for them, and re-layouts  74.8 us (19%)
  matrix products  44.8 us (11%)
  other arithmetic  39.6 us (10%)
  loops' own time  33.4 us (8%)
  between operations  29.4 us (7%)
  starting transfers between devices  22.5 us (6%)
  blocking collectives  17.1 us (4%)
    all_gather x1, waiting for transfers between devices, entering(): pieces = jax.tree.map(lambda part: lax.all_gather(part, axis), value)  69.7 us
    psum x1, waiting for transfers between devices, spread(): return lax.psum(kept, axis)  57.4 us
    unnamed x45, local copies, waits for them, and re-layouts  35.1 us
    another operation x1, loops' own time, entering(): return lax.fori_loop(0, count - 1, lap, so_far)  33.4 us
    dot_general x3, matrix products, direct_part(): jnp.einsum('hqk,khd->qhd', weights, value_rows, preferred_element_type=jn...  29.3 us
    ppermute x6, starting transfers between devices, shifted(): return lax.ppermute(value, axis, pairs)  22.5 us
    select_n x7, other arithmetic, lap(): jnp.where(position < mine, new, old)  12.2 us
    reshape x3, local copies, waits for them, and re-layouts, finish(): normed.astype(jnp.bfloat16).reshape(query_rows.shape[0], HEADS * HEAD)  10.8 us
  transfers between devices with their start and end apart: 8, of which 5 were waited for; matrix products, arithmetic and copies ran while one was open for 13% of the time, Pallas kernels for 0%

commit v1 on v0

--- a/solution.py
+++ b/solution.py
@@ -8,6 +8,9 @@
 HEAD = 128
 TILE = 128
 BLOCK = 512
+turn_lots_all = lambda content, ax_name: jnp.sum(
+    jax.lax.all_gather(content, axis_name=ax_name), axis=0
+)
 
 
 def shifted(value, axis, by):
@@ -32,7 +35,7 @@
 
 def spread(value, axis, source):
     kept = jnp.where(lax.axis_index(axis) == source, value, 0).astype(value.dtype)
-    return lax.psum(kept, axis)
+    return turn_lots_all(kept, ax_name=axis)
 
 
 def combine(first, second):

time: 399 us -> 422 us (1.058)
  waiting for transfers between devices: 136 us -> 159 us
  other arithmetic: 39.6 us -> 46.2 us
    all_gather x0 -> x1, waiting for transfers between devices: none -> 80.7 us  [jax.lax.all_gather(content, axis_name=ax_name)]
    psum x1 -> x0, waiting for transfers between devices: 57.4 us -> none  [spread(): return lax.psum(kept, axis)]
    psum x1 -> x0, blocking collectives: 7.79 us -> none  [spread(): return lax.psum(kept, axis)]
    unnamed x1 -> x2, blocking collectives: 9.27 us -> 16 us
    reduce_sum x0 -> x3, other arithmetic: none -> 5.5 us  [jnp.sum(jax.lax.all_gather(content, axis_name=ax_name), axis=0)]
where the time goes in v1:
time: 422 us; the launch traced here: 420 us
  waiting for transfers between devices  159 us (38%)
  local copies, waits for them, and re-layouts  74.3 us (18%)
  other arithmetic  46.2 us (11%)
  matrix products  45 us (11%)
  loops' own time  29.5 us (7%)
  between operations  27.9 us (7%)
  starting transfers between devices  22.2 us (5%)
  blocking collectives  16 us (4%)
    all_gather x1, waiting for transfers between devices, jax.lax.all_gather(content, axis_name=ax_name)  80.7 us
    all_gather x1, waiting for transfers between devices, entering(): pieces = jax.tree.map(lambda part: lax.all_gather(part, axis), value)  69.7 us
    unnamed x45, local copies, waits for them, and re-layouts  35.4 us
    dot_general x3, matrix products, direct_part(): jnp.einsum('hqk,khd->qhd', weights, value_rows, preferred_element_type=jn...  29.9 us
    another operation x1, loops' own time, entering(): return lax.fori_loop(0, count - 1, lap, so_far)  29.5 us
    ppermute x6, starting transfers between devices, shifted(): return lax.ppermute(value, axis, pairs)  22.1 us
    unnamed x2, blocking collectives  16 us
    select_n x7, other arithmetic, lap(): jnp.where(position < mine, new, old)  12.2 us
  transfers between devices with their start and end apart: 8, of which 5 were waited for; matrix products, arithmetic and copies ran while one was open for 13% of the time, Pallas kernels for 0%

profile of v1, /device:TPU:4, one launch (start us, length us, event | category | flops | bytes accessed | tf_op | source)
XLA Modules:
  0.0 419.7 jit_solution(13937355104642246741)
XLA Ops:
  16.4 5.8 %fusion.54 = (bf16[512,2048]{1,0:T(8,128)(2,1)}, bf16[512,2048]{1,0:T(8,128)(2,1)S(1)}, bf16[512,2048]{1,0:T(8,128)(2,1)}) fusion(bf16[1536,2048]{1,0:T(8,128)(2,1)} %param.9), kind=kLoop, calls=%fused_computation.96 | loop fusion | bytes 12582912 | tf_op jit(solution)/shard_map/slice | solution.py:126
  22.2 4.0 copy.108
  26.2 5.8 %fusion.55 = (bf16[512,2048]{1,0:T(8,128)(2,1)}, bf16[512,2048]{1,0:T(8,128)(2,1)}, bf16[512,2048]{1,0:T(8,128)(2,1)}) fusion(bf16[1536,2048]{1,0:T(8,128)(2,1)} %param.10), kind=kLoop, calls=%fused_computation.97 | loop fusion | bytes 12582912 | tf_op jit(solution)/shard_map/slice | solution.py:127
  32.0 4.0 copy.69
  35.9 3.9 copy.111
  46.3 4.1 copy.110
  61.8 9.3 %all-reduce.5 = (s32[8]{0:T(128)S(1)}, s32[8]{0:T(128)S(1)}) all-reduce(s32[8]{0:T(128)S(1)} %dynamic-update-slice, s32[8]{0:T(128)S(1)} %dynamic-update-slice.1), channel_id=2, replica_groups=mesh['outer'=4,'inner'=8] {'inner'}, use_global_device_ids=true, to_apply=%add | all-reduce | flops 16 | bytes 128
  71.0 69.7 %all-gather.9.cloned.1.call-done = f32[128,128,128]{2,1,0:T(8,128)} async-done(((f32[16,128,128]{2,1,0:T(8,128)}), f32[128,128,128]{2,1,0:T(8,128)}) %all-gather.9.cloned.1.call-update) | async-done | bytes 8388624 | tf_op jit(solution)/shard_map/all_gather | solution.py:24
  140.7 50.2 %while.18 = (s32[]{:T(128)}, f32[16,128,128]{2,1,0:T(8,128)S(1)}, s32[1]{0:T(128)}, s32[1]{0:T(128)}, s32[]{:T(128)}, /*index=5*/s32[8,1]{0,1:T(1,128)S(1)}, s32...) while((s32[]{:T(128)}, f32[16,128,128]{2,1,0:T(8,128)S(1)}, ...), condition=%wide.region_1.2_spmd.clone, body=%wide.region_0.1_spmd.clone.sunk | while | flops 1048594 | bytes 3146019 | solution.py:33
  192.7 80.7 %all-gather.11.cloned.1.call-done = f32[128,128,128]{2,1,0:T(8,128)} async-done(((f32[16,128,128]{2,1,0:T(8,128)}), f32[128,128,128]{2,1,0:T(8,128)}) %all-gather.11.cloned.1.call-update) | async-done | bytes 8388624 | tf_op jit(solution)/shard_map/all_gather | solution.py:12
  273.3 4.2 reduce_sum.59
  282.0 5.7 %fusion.53 = (bf16[512,2048]{1,0:T(8,128)(2,1)}, bf16[512,2048]{1,0:T(8,128)(2,1)}, bf16[512,2048]{1,0:T(8,128)(2,1)}) fusion(bf16[1536,2048]{1,0:T(8,128)(2,1)} %param.8), kind=kLoop, calls=%fused_computation.95 | loop fusion | bytes 12582912 | tf_op jit(solution)/shard_map/slice | solution.py:125
  289.8 3.9 copy.114
  293.7 6.8 %all-reduce.4 = (s32[8]{0:T(128)S(1)}, s32[8]{0:T(128)S(1)}) all-reduce(s32[8]{0:T(128)S(1)} %select_dynamic-update-slice_fusion.1, s32[8]{0:T(128)S(1)} %select_dynamic-update-slice_fusion), channel_id=5, replica_groups=mesh['outer'=4,'inner'=8] {'inner'}, use_global_device_ids=true, to_apply=%add.2 | all-reduce | flops 16 | bytes 128
  314.6 10.0 %fusion.6 = f32[16,512,128]{1,2,0:T(8,128)} fusion(bf16[512,16,128]{0,2,1:T(8,128)(2,1)} %bitcast.162, bf16[512,16,128]{0,2,1:T(8,128)(2,1)} %bitcast.141, bf16[512,16,128]{0,2,1:T(8,128)(2,1)} %bitcast.160, pred[512,512]{1,0:T(8,128)(4,1)} %get-tuple-element.236), kind=kOutput, calls=%fused_computation.22 | convolution fusion | flops 2155872256 | bytes 10747904 | tf_op jit(solution)/shard_map/hqk,khd->qhd/dot_general | solution.py:78
  324.5 3.9 copy.113
  328.5 3.9 copy.107
  333.3 9.9 %fusion.5 = f32[16,512,128]{1,2,0:T(8,128)} fusion(bf16[512,16,128]{0,2,1:T(8,128)(2,1)} %bitcast.158, bf16[512,16,128]{0,2,1:T(8,128)(2,1)} %bitcast.146, bf16[512,16,128]{0,2,1:T(8,128)(2,1)} %bitcast.156, pred[512,512]{1,0:T(8,128)(4,1)S(1)} %get-tuple-element.235), kind=kOutput, calls=%fused_computation.21 | convolution fusion | flops 2155872256 | bytes 10747904 | tf_op jit(solution)/shard_map/hqk,khd->qhd/dot_general | solution.py:78
  356.4 10.0 %fusion.4 = f32[16,512,128]{1,2,0:T(8,128)} fusion(bf16[512,16,128]{0,2,1:T(8,128)(2,1)} %bitcast.155, bf16[512,16,128]{0,2,1:T(8,128)(2,1)} %bitcast.143, bf16[512,16,128]{0,2,1:T(8,128)(2,1)} %bitcast.152, pred[512,512]{1,0:T(8,128)(4,1)S(1)} %copy-done.12), kind=kOutput, calls=%fused_computation.20 | convolution fusion | flops 2155872256 | bytes 10747904 | tf_op jit(solution)/shard_map/hqk,khd->qhd/dot_general | solution.py:78
  367.7 8.3 %collective-permute-start.2 = (s32[1]{0:T(128)}, s32[1]{0:T(128)}, u32[]{:S(2)}, u32[]{:S(2)}) collective-permute-start(s32[1]{0:T(128)} %select_n.311), channel_id=1, source_target_pairs={{0,8},{8,16},{16,24},{1,9},{9,17},{17,25},{2,10},{10,18},{18,26},{... | collective-permute-start | bytes 20 | tf_op jit(solution)/shard_map/ppermute | solution.py:19
  382.4 4.9 %multiply_reduce_fusion = (f32[512,16]{0,1:T(8,128)S(1)}, f32[512,16,128]{0,2,1:T(8,128)S(1)}) fusion(bf16[512,16,128]{0,2,1:T(8,128)(2,1)S(1)} %bitcast.142, f32[16,128,128]{2,1,0:T(8,128)S(1)} %fusion.9, f32[16,128,128]{2,1,0:T(8,128)S(1)} %add_select_fusion.2, pred[]{:T(512)S(6)} %or.47, pred[512]{0:T(512)(128)(4,1)S(1)} %get-tuple-element.234, ...), kind=kOutput, calls=%fused_computation.15 | convolution fusion | flops 1616371712 | bytes 12616705 | tf_op jit(solution)/shard_map/qhd,hde->qhe/dot_general | solution.py:83
  399.5 4.0 copy.90
  403.5 4.0 copy.91
  407.5 5.4 %pad_maximum_fusion = bf16[1536,2048]{1,0:T(8,128)(2,1)} fusion(bf16[512,2048]{1,0:T(8,128)(2,1)} %copy.91, bf16[512,2048]{1,0:T(8,128)(2,1)} %copy.90, bf16[512,2048]{1,0:T(8,128)(2,1)S(1)} %copy.89), kind=kLoop, calls=%fused_computation.7 | loop fusion | flops 18874368 | bytes 12582912 | tf_op jit(solution)/shard_map/concatenate | solution.py:162
  (108 shorter events, 90.3 us)
Async XLA Ops:
  6.5 134.2 %all-gather.9.cloned.1.call-start = ((), (), s32[]{:S(2)}) async-start(), calls=%async_computation | async-start | bytes 9437184 | tf_op jit(solution)/shard_map/all_gather | solution.py:24
  46.3 4.1 copy-start.6
  50.4 2.5 copy-start.7
  50.4 2.9 copy-start.8
  52.8 1.1 copy-start.11
  53.2 1.6 copy-start.9
  53.2 2.2 copy-start.10
  55.4 3.0 copy-start.14
  57.2 216.1 %all-gather.11.cloned.1.call-start = ((), (), s32[]{:S(2)}) async-start(), calls=%async_computation.1 | async-start | bytes 9437184 | tf_op jit(solution)/shard_map/all_gather | solution.py:12
  140.7 50.8 %copy-start.5 = (f32[16,128,128]{2,1,0:T(8,128)S(1)}, f32[16,128,128]{2,1,0:T(8,128)}, u32[]{:S(2)}) copy-start(f32[16,128,128]{2,1,0:T(8,128)} %add_select_fusion.7) | copy-start | bytes 3145732
  277.5 32.5 %collective-permute-start.3 = (f32[16,128,128]{2,1,0:T(8,128)S(1)}, f32[16,128,128]{2,1,0:T(8,128)}, u32[]{:S(2)}, u32[]{:S(2)}) collective-permute-start(f32[16,128,128]{2,1,0:T(8,128)S(1)} %reduce_sum.59), channel_id=1, source_target_pairs={{0,8},{8,16},{16,24},{1,9},{9,17},{17,25},{2,10},{10,18},{18,26},{... | collective-permute-start | bytes 3145736 | tf_op jit(solution)/shard_map/ppermute | solution.py:19
  302.4 6.4 %collective-permute-start = (s32[1]{0:T(128)}, s32[1]{0:T(128)}, u32[]{:S(2)}, u32[]{:S(2)}) collective-permute-start(s32[1]{0:T(128)} %select_n.309), channel_id=1, source_target_pairs={{0,8},{8,16},{16,24},{1,9},{9,17},{17,25},{2,10},{10,18},{18,26},{... | collective-permute-start | bytes 20 | tf_op jit(solution)/shard_map/ppermute | solution.py:19
  312.5 39.7 %collective-permute-start.4 = (f32[16,128,128]{2,1,0:T(8,128)}, f32[16,128,128]{2,1,0:T(8,128)}, u32[]{:S(2)}, u32[]{:S(2)}) collective-permute-start(f32[16,128,128]{2,1,0:T(8,128)} %add_select_fusion.5), channel_id=1, source_target_pairs={{0,8},{8,16},{16,24},{1,9},{9,17},{17,25},{2,10},{10,18},{18,26},{... | collective-permute-start | bytes 3145736 | tf_op jit(solution)/shard_map/ppermute | solution.py:19
  343.3 13.1 %copy-start.12 = (pred[512,512]{1,0:T(8,128)(4,1)S(1)}, pred[512,512]{1,0:T(8,128)(4,1)}, u32[]{:S(2)}) copy-start(pred[512,512]{1,0:T(8,128)(4,1)} %fusion.25) | copy-start | bytes 786436
  344.5 6.3 %collective-permute-start.1 = (s32[1]{0:T(128)}, s32[1]{0:T(128)}, u32[]{:S(2)}, u32[]{:S(2)}) collective-permute-start(s32[1]{0:T(128)} %select_n.310), channel_id=1, source_target_pairs={{0,8},{8,16},{16,24},{1,9},{9,17},{17,25},{2,10},{10,18},{18,26},{... | collective-permute-start | bytes 20 | tf_op jit(solution)/shard_map/ppermute | solution.py:19
  354.5 26.0 %collective-permute-start.5 = (f32[16,128,128]{2,1,0:T(8,128)}, f32[16,128,128]{2,1,0:T(8,128)S(1)}, u32[]{:S(2)}, u32[]{:S(2)}) collective-permute-start(f32[16,128,128]{2,1,0:T(8,128)} %add_select_fusion.4), channel_id=1, source_target_pairs={{0,8},{8,16},{16,24},{1,9},{9,17},{17,25},{2,10},{10,18},{18,26},{... | collective-permute-start | bytes 3145736 | tf_op jit(solution)/shard_map/ppermute | solution.py:19
  367.7 11.5 %collective-permute-start.2 = (s32[1]{0:T(128)}, s32[1]{0:T(128)}, u32[]{:S(2)}, u32[]{:S(2)}) collective-permute-start(s32[1]{0:T(128)} %select_n.311), channel_id=1, source_target_pairs={{0,8},{8,16},{16,24},{1,9},{9,17},{17,25},{2,10},{10,18},{18,26},{... | collective-permute-start | bytes 20 | tf_op jit(solution)/shard_map/ppermute | solution.py:19
  380.5 1.9 copy-start.1
  382.4 5.0 %copy-start.3 = (bf16[512,2048]{0,1:T(8,128)(2,1)S(1)}, bf16[512,2048]{0,1:T(8,128)(2,1)}, u32[]{:S(2)}) copy-start(bf16[512,2048]{0,1:T(8,128)(2,1)} %copy.113) | copy-start | bytes 6291460
  382.4 5.0 %copy-start.4 = (f32[16,512,128]{1,2,0:T(8,128)S(1)}, f32[16,512,128]{1,2,0:T(8,128)}, u32[]{:S(2)}) copy-start(f32[16,512,128]{1,2,0:T(8,128)} %fusion.5) | copy-start | bytes 12582916
  387.4 2.6 copy-start
  387.4 2.9 copy-start.2
  390.3 2.7 copy-start.13
Sparse Core Ops, SparseCore 0:
  57.3 83.3 all-gather.8
  192.8 80.4 all-gather.10
